TPU v7x, 32 devices: a whole 2x2x4 slice. The times are simulated.
32 devices in a mesh: dp: 4 (over y, x), seq: 8 (over z, core).
Axes of the slice: x: 2, y: 2, z: 4, core: 2. Of those that a mesh axis runs over, the one named last changes fastest.
Arguments:
- binned_signals: bfloat16 [4, 4096, 768], P('dp', 'seq'), may hold values from -6 to 6
- kernel_coefficients: bfloat16 [5, 768, 768], P(None, 'dp'), may hold values from -0.09375 to 0.09375
- asking_projector: bfloat16 [768, 256], replicated, may hold values from -0.21875 to 0.21875
- lookup_projector: bfloat16 [768, 256], replicated, may hold values from -0.21875 to 0.21875
- content_projector: bfloat16 [768, 384], replicated, may hold values from -0.21875 to 0.21875
- readout_projector: bfloat16 [384, 768], replicated, may hold values from -0.3125 to 0.3125
- logit_multipliers: float32 [4], replicated, may hold values from 8 to 24
- loss_sensitivity: bfloat16 [4, 1024, 768], P('dp', 'seq'), may hold values from -0.09375 to 0.09375
Outputs:
- pooled: bfloat16 [4, 1024, 768], P('dp', 'seq')
- update: float32 [4, 1024, 768], P('dp', 'seq')
- query_grad: float32 [768, 256], replicated
- out_grad: float32 [384, 768], replicated
All inputs are finite; a program needn't handle non-finite values.
Results may differ from a plain program's by a relative error of at most 0.0095.
The roundings to bfloat16 on the way count: a program that leaves them out, or rounds other values in their place, can miss the bound.
Values may be sent and summed in bfloat16 or wider, within the bound.
A program may use at most 128 MiB of HBM per device.

v0:
```python
import jax
import jax.numpy as jnp
from jax import lax
from jax.sharding import PartitionSpec as P

POOL = 4


norm_eps = 1e-05
head_eps = 1e-06


def padded_2(array, sides, width):
    for axis, dim in sides:
        devices, length = (lax.axis_size(axis), array.shape[dim])
        up = [(i, (i + 1) % devices) for i in range(devices - 1)]
        down = [(j, i) for i, j in up]
        last = lax.slice_in_dim(array, length - width, length, axis=dim)
        leading = lax.slice_in_dim(array, 0, width, axis=dim)
        before = lax.ppermute(last, axis, up)
        after = lax.ppermute(leading, axis, down)
        array = jnp.concatenate([before, array, after], axis=dim)
    return array


def layer_norm(values):
    centre = jnp.mean(values, axis=-1, keepdims=True)
    shifted = values - centre
    variance = jnp.mean(shifted * shifted, axis=-1, keepdims=True)
    return shifted * lax.rsqrt(variance + norm_eps)


def activate(values):
    return values * jax.nn.sigmoid(1.702 * values)


def head_norm(values, group_width):
    grouped = values.reshape(values.shape[0], -1, group_width)
    factor = lax.rsqrt(jnp.mean(grouped * grouped, axis=-1, keepdims=True) + head_eps)
    return (
        (grouped * factor).reshape(values.shape),
        jnp.broadcast_to(factor, grouped.shape).reshape(values.shape),
    )


def contract_first(former, latter):
    return lax.dot_general(
        former, latter, (((0,), (0,)), ((), ())), preferred_element_type=jnp.float32
    )


def contract_last(former, latter):
    return lax.dot_general(
        former, latter, (((1,), (1,)), ((), ())), preferred_element_type=jnp.float32
    )


def stacked_conv(padded, all_taps, length_fine):
    tap_count = all_taps.shape[0]
    windows = jnp.concatenate(
        [padded[tap_index : tap_index + length_fine] for tap_index in range(tap_count)], axis=1
    )
    flat_taps = all_taps.reshape(tap_count * all_taps.shape[1], all_taps.shape[2])
    return jnp.dot(windows, flat_taps, preferred_element_type=jnp.float32)


def on_device(
    binned_signals,
    kernel_coefficients,
    asking_projector,
    lookup_projector,
    content_projector,
    readout_projector,
    logit_multipliers,
    loss_sensitivity,
):
    incoming_tensor = binned_signals[0]
    directional_perturbations = loss_sensitivity[0]
    length_fine = incoming_tensor.shape[0]
    channels = incoming_tensor.shape[1]
    tap_count = kernel_coefficients.shape[0]
    margin = tap_count // 2
    attender_total = logit_multipliers.shape[0]
    probe_extent = asking_projector.shape[1] // attender_total
    value_width = content_projector.shape[1] // attender_total
    activated = activate(layer_norm(incoming_tensor.astype(jnp.float32))).astype(jnp.bfloat16)
    padded = padded_2(activated, (("seq", 0),), margin)
    all_taps = lax.all_gather(kernel_coefficients, "dp", axis=1, tiled=True)
    conv_sum = stacked_conv(padded, all_taps, length_fine)
    summed = incoming_tensor.astype(jnp.float32) + conv_sum
    pooled = jnp.max(summed.reshape(length_fine // POOL, POOL, channels), axis=1).astype(
        jnp.bfloat16
    )
    normed = layer_norm(pooled.astype(jnp.float32)).astype(jnp.bfloat16)
    queries = jnp.dot(normed, asking_projector, preferred_element_type=jnp.float32)
    query_hat, query_factor = head_norm(queries, probe_extent)
    query_unit = query_hat.astype(jnp.bfloat16)
    key_local = head_norm(
        jnp.dot(normed, lookup_projector, preferred_element_type=jnp.float32), probe_extent
    )[0].astype(jnp.bfloat16)
    value_local = jnp.dot(normed, content_projector, preferred_element_type=jnp.float32).astype(
        jnp.bfloat16
    )
    key_unit, values_all = (
        lax.all_gather(key_local, "seq", axis=0, tiled=True),
        lax.all_gather(value_local, "seq", axis=0, tiled=True),
    )
    heads_grad = contract_last(directional_perturbations, readout_projector).astype(jnp.bfloat16)
    outputs = []
    diffs = []
    for attender_slot in range(attender_total):
        key_lo = attender_slot * probe_extent
        value_lo = attender_slot * value_width
        query_part = query_unit[:, key_lo : key_lo + probe_extent]
        key_part = key_unit[:, key_lo : key_lo + probe_extent]
        value_part = values_all[:, value_lo : value_lo + value_width]
        attender_logit_gain = logit_multipliers[attender_slot] / probe_extent
        scores = contract_last(query_part, key_part) * attender_logit_gain
        expo = jnp.exp(scores)
        probs = expo / jnp.sum(expo, axis=1, keepdims=True)
        head_out = jnp.dot(
            probs.astype(jnp.bfloat16), value_part, preferred_element_type=jnp.float32
        )
        outputs.append(head_out)
        grad_part = heads_grad[:, value_lo : value_lo + value_width]
        prob_grad = contract_last(grad_part, value_part)
        delta = jnp.sum(grad_part.astype(jnp.float32) * head_out, axis=1, keepdims=True)
        score_grad = (probs * (prob_grad - delta)).astype(jnp.bfloat16)
        unit_grad = (
            jnp.dot(score_grad, key_part, preferred_element_type=jnp.float32) * attender_logit_gain
        )
        hat_part = query_hat[:, key_lo : key_lo + probe_extent]
        factor_part = query_factor[:, key_lo : key_lo + probe_extent]
        diffs.append(
            factor_part
            * (unit_grad - hat_part * jnp.mean(hat_part * unit_grad, axis=1, keepdims=True))
        )
    heads_low = jnp.concatenate(outputs, axis=1).astype(jnp.bfloat16)
    update = jnp.dot(heads_low, readout_projector, preferred_element_type=jnp.float32)
    query_diff = jnp.concatenate(diffs, axis=1).astype(jnp.bfloat16)
    query_local = contract_first(normed, query_diff)
    out_local = contract_first(heads_low, directional_perturbations)
    query_grad, out_grad = lax.psum((query_local, out_local), ("dp", "seq"))
    return (pooled[None], update[None], query_grad, out_grad)


def solution(mesh):
    return jax.shard_map(
        on_device,
        mesh=mesh,
        in_specs=(
            P("dp", "seq", None),
            P(None, "dp", None),
            P(),
            P(),
            P(),
            P(),
            P(),
            P("dp", "seq", None),
        ),
        out_specs=(P("dp", "seq", None), P("dp", "seq", None), P(), P()),
        check_vma=False,
    )
```

profile of v0, /device:TPU:0, one launch (start us, length us, event | category | flops | bytes accessed | tf_op | source)
XLA Modules:
  0.0 278.9 jit_solution(9412636487613253405)
XLA Ops:
  7.2 0.0 copy-start
  7.2 0.0 all-gather.2.cloned.1.call-start
  7.2 0.7 all-gather.2.cloned.1.call-update
  7.9 0.0 all-reduce.3.cloned.1.call-start
  8.0 0.4 copy-done.1
  8.4 0.2 convert_reduce_fusion
  8.6 0.0 copy-start.10
  8.6 0.4 fusion.11
  8.9 0.6 fusion.10
  9.6 2.4 collective-permute-start
  11.9 1.3 collective-permute-start.1
  13.2 0.0 copy-done
  13.2 0.0 copy-done.4
  13.2 0.3 convolution_convert_fusion
  13.6 0.6 fusion.112
  16.8 0.0 collective-permute-done
  16.8 1.1 fusion.35
  17.9 1.1 fusion.37
  19.0 1.5 constant_dynamic-update-slice_fusion
  20.6 0.0 collective-permute-done.1
  20.6 1.1 fusion.33
  21.7 1.2 fusion.36
  22.9 56.6 %all-gather.2.cloned.1.call-done = bf16[5,768,768]{2,1,0:T(8,128)(2,1)} async-done(((bf16[5,192,768]{2,1,0:T(8,128)(2,1)}), bf16[5,768,768]{2,1,0:T(8,128)(2,1)}) %all-gather.2.cloned.1.call-update) | async-done | bytes 5898256 | tf_op jit(solution)/shard_map/all_gather | solution.py:88
  79.5 7.1 %fusion = bf16[512,768]{1,0:T(8,128)(2,1)S(1)} fusion(bf16[1,512,768]{2,1,0:T(8,128)(2,1)S(1)} %copy-done.1, bf16[512,3840]{1,0:T(8,128)(2,1)} %fusion.36, bf16[3840,768]{1,0:T(8,128)(2,1)} %bitcast.59), kind=kOutput, calls=%fused_computation.2 | convolution fusion | flops 3021078528 | bytes 11403264 | tf_op jit(solution)/shard_map/dot_general | solution.py:64
  86.6 0.0 copy-start.8
  86.6 0.2 reshape.105
  86.8 0.0 copy-start.9
  86.8 1.0 reduce_max.9
  87.8 0.0 copy-start.2
  87.8 0.1 convert_reduce_fusion.1
  88.0 0.2 fusion.40
  88.2 0.3 fusion.114
  88.5 0.1 copy.17
  88.6 0.1 copy.18
  88.7 0.3 fusion.113
  89.0 0.1 copy.19
  89.2 0.1 copy.20
  89.3 0.0 copy-start.11
  89.3 14.9 %all_gather.10 = bf16[1024,256]{1,0:T(8,128)(2,1)S(1)} all-gather(bf16[128,256]{1,0:T(8,128)(2,1)S(1)} %multiply_convert_fusion), channel_id=1, replica_groups=mesh['dp'=4,'seq'=8] {'seq'}, dimensions={0}, use_global_device_ids=true | all-gather | bytes 589824 | tf_op jit(solution)/shard_map/all_gather | solution.py:105
  104.2 0.3 fusion.115
  104.5 0.4 fusion.118
  105.0 0.0 copy-start.5
  105.0 0.3 convolution_convert_fusion.1
  105.3 15.8 %all_gather.11 = bf16[1024,384]{1,0:T(8,128)(2,1)S(1)} all-gather(bf16[128,384]{1,0:T(8,128)(2,1)S(1)} %convolution_convert_fusion.1), channel_id=1, replica_groups=mesh['dp'=4,'seq'=8] {'seq'}, dimensions={0}, use_global_device_ids=true | all-gather | bytes 884736 | tf_op jit(solution)/shard_map/all_gather | solution.py:106
  121.1 0.3 fusion.117
  121.4 0.4 fusion.116
  121.9 0.4 fusion.46
  122.3 0.4 fusion.48
  122.7 0.4 fusion.50
  123.1 0.9 multiply_reduce_fusion.7
  124.0 1.5 fusion.30
  125.5 1.5 fusion.29
  127.0 1.5 fusion.28
  128.6 1.7 multiply_reduce_fusion.3
  130.3 0.7 broadcast_multiply_fusion.1
  131.0 0.7 broadcast_multiply_fusion.3
  131.6 1.3 fusion.74
  133.0 0.2 fusion.80
  133.2 1.3 fusion.81
  134.4 0.0 all-reduce.3.cloned.1.call-update
  134.5 1.0 convolution_bitcast_fusion
  135.5 133.4 %all-reduce.3.cloned.1.call-done = (f32[768,256]{1,0:T(8,128)}, f32[384,768]{1,0:T(8,128)}) async-done(((f32[768,256]{1,0:T(8,128)}, f32[384,768]{1,0:T(8,128)}), (f32[768,256]{1,0:T(8,128)}, f32[384,768]{1,0:T(8,128)})) %all-reduce.3.cloned.1.call-update) | async-done | bytes 1966096 | tf_op jit(solution)/shard_map/psum | solution.py:143
  268.9 2.2 copy.41
  271.0 1.0 copy.42
  (27 shorter events, 0.2 us)
Async XLA Ops:
  7.2 6.1 %copy-start = (bf16[384,768]{1,0:T(8,128)(2,1)S(1)}, bf16[384,768]{1,0:T(8,128)(2,1)}, u32[]{:S(2)}) copy-start(bf16[384,768]{1,0:T(8,128)(2,1)} %param.13) | copy-start | bytes 1769476
  7.2 1.2 copy-start.1
  7.2 72.3 %all-gather.2.cloned.1.call-start = ((), (), s32[]{:S(2)}) async-start(), calls=%async_computation | async-start | bytes 7372800 | tf_op jit(solution)/shard_map/all_gather | solution.py:88
  7.9 5.3 %copy-start.4 = (bf16[1,128,768]{2,1,0:T(8,128)(2,1)S(1)}, bf16[1,128,768]{2,1,0:T(8,128)(2,1)}, u32[]{:S(2)}) copy-start(bf16[1,128,768]{2,1,0:T(8,128)(2,1)} %param.15) | copy-start | bytes 589828
  7.9 260.9 %all-reduce.3.cloned.1.call-start = ((), (), s32[]{:S(2)}) async-start(), calls=%async_computation.1 | async-start | bytes 3932160 | tf_op jit(solution)/shard_map/psum | solution.py:143
  8.6 5.0 %copy-start.10 = (f32[4]{0:T(128)S(1)}, f32[4]{0:T(128)}, u32[]{:S(2)}) copy-start(f32[4]{0:T(128)} %param.14) | copy-start | bytes 52
  9.6 7.2 %collective-permute-start = (bf16[2,768]{1,0:T(2,128)(2,1)S(1)}, bf16[2,768]{1,0:T(2,128)(2,1)S(1)}, u32[]{:S(2)}, u32[]{:S(2)}) collective-permute-start(bf16[2,768]{1,0:T(2,128)(2,1)S(1)} %get-tuple-element.17), channel_id=1, source_target_pairs={{0,1},{1,2},{2,3},{3,4},{4,5},{5,6},{6,7},{8,9},{9,10},{10,11},{11... | collective-permute-start | bytes 9224 | tf_op jit(solution)/shard_map/ppermute | solution.py:20
  11.9 8.7 %collective-permute-start.1 = (bf16[2,768]{1,0:T(2,128)(2,1)S(1)}, bf16[2,768]{1,0:T(2,128)(2,1)S(1)}, u32[]{:S(2)}, u32[]{:S(2)}) collective-permute-start(bf16[2,768]{1,0:T(2,128)(2,1)S(1)} %get-tuple-element.16), channel_id=1, source_target_pairs={{1,0},{2,1},{3,2},{4,3},{5,4},{6,5},{7,6},{9,8},{10,9},{11,10},{12... | collective-permute-start | bytes 9224 | tf_op jit(solution)/shard_map/ppermute | solution.py:21
  86.6 1.6 copy-start.8
  86.8 2.0 copy-start.9
  87.8 45.3 %copy-start.2 = (bf16[128,768]{1,0:T(8,128)(2,1)}, bf16[128,768]{1,0:T(8,128)(2,1)S(1)}, u32[]{:S(2)}) copy-start(bf16[128,768]{1,0:T(8,128)(2,1)S(1)} %reduce_max.9) | copy-start | bytes 589828
  89.3 15.7 %copy-start.11 = (bf16[768,384]{1,0:T(8,128)(2,1)S(1)}, bf16[768,384]{1,0:T(8,128)(2,1)}, u32[]{:S(2)}) copy-start(bf16[768,384]{1,0:T(8,128)(2,1)} %param.12) | copy-start | bytes 1769476
  105.0 16.9 %copy-start.5 = (f32[128,1024]{1,0:T(8,128)}, f32[128,1024]{1,0:T(8,128)S(1)}, u32[]{:S(2)}) copy-start(f32[128,1024]{1,0:T(8,128)S(1)} %get-tuple-element.41) | copy-start | bytes 1572868
  121.4 1.2 copy-start.6
  121.8 0.8 copy-start.7
  268.9 2.2 copy-start.3
Sparse Core Ops, SparseCore 0:
  9.9 69.5 all-gather.1
  134.6 134.2 all-reduce.2
where the time goes:
time: 279 us
  waiting for transfers between devices  191 us (68%)
  blocking collectives  30.7 us (11%)
  matrix products  21.7 us (8%)
  between operations  17 us (6%)
  other arithmetic  10.2 us (4%)
  local copies, waits for them, and re-layouts  4.8 us (2%)
  starting transfers between devices  3.72 us (1%)
    psum x1, waiting for transfers between devices, on_device(): query_grad, out_grad = lax.psum((query_local, out_local), ('dp', 'seq'))  133 us
    all_gather x1, waiting for transfers between devices, on_device(): all_taps = lax.all_gather(kernel_coefficients, 'dp', axis=1, tiled=True)  56.6 us
    all_gather x1, blocking collectives, on_device(): lax.all_gather(value_local, 'seq', axis=0, tiled=True)  15.8 us
    all_gather x1, blocking collectives, on_device(): lax.all_gather(key_local, 'seq', axis=0, tiled=True)  14.9 us
    dot_general x1, matrix products, stacked_conv(): return jnp.dot(windows, flat_taps, preferred_element_type=jnp.float32)  7.07 us
    dot_general x4, matrix products, on_device(): jnp.dot(score_grad, key_part, preferred_element_type=jnp.float32)  6.29 us
  transfers between devices with their start and end apart: 4, of which 2 were waited for; matrix products, arithmetic and copies ran while one was open for 3% of the time, Pallas kernels for 0%

commit v1 on v0

v1 whole, which is shorter than its diff:
```python
import functools
import math

import jax
import jax.numpy as jnp
from jax import lax
from jax.experimental import pallas as pl
from jax.experimental.pallas import tpu as pltpu
from jax.sharding import PartitionSpec as P

POOL = 4
LANES = 128
norm_eps = 1e-05
head_eps = 1e-06
F32 = jnp.float32
BF16 = jnp.bfloat16
MESH = pl.DeviceIdType.MESH


def layer_norm(values):
    centre = jnp.mean(values, axis=-1, keepdims=True)
    shifted = values - centre
    variance = jnp.mean(shifted * shifted, axis=-1, keepdims=True)
    return shifted * lax.rsqrt(variance + norm_eps)


def dot(a, b):
    return lax.dot_general(a, b, (((1,), (0,)), ((), ())), preferred_element_type=F32)


def dot_last(a, b):
    return lax.dot_general(a, b, (((1,), (1,)), ((), ())), preferred_element_type=F32)


def dot_first(a, b):
    return lax.dot_general(a, b, (((0,), (0,)), ((), ())), preferred_element_type=F32)


def head_masks(rows, width, heads):
    lane = lax.broadcasted_iota(jnp.int32, (rows, width), 1)
    size = width // heads
    return [(lane >= h * size) & (lane < (h + 1) * size) for h in range(heads)]


def head_sums(values, masks):
    return [jnp.sum(jnp.where(m, values, 0.0), axis=1, keepdims=True) for m in masks]


def spread(columns, masks):
    total = jnp.zeros(masks[0].shape, F32)
    for column, m in zip(columns, masks):
        total = jnp.where(m, column, total)
    return total


def kernel(
    n_dp,
    n_seq,
    part,
    x_ref,
    taps_ref,
    ask_ref,
    look_ref,
    content_ref,
    read_ref,
    gain_ref,
    sens_ref,
    pooled_ref,
    update_ref,
    grads_ref,
    taps,
    x_wide,
    act,
    phases,
    kv,
    grads,
    grads_low,
    from_core,
    from_dp,
    from_z,
    low_dp,
    low_z,
    result,
    tap_send,
    tap_recv,
    tap_core_send,
    tap_core_recv,
    own_sem,
    halo_send,
    halo_recv,
    kv_send,
    kv_recv,
    kv_core_send,
    kv_core_recv,
    dp_send,
    dp_recv,
    z_send,
    z_recv,
    core_send,
    core_recv,
):
    d = lax.axis_index("dp")
    seq = lax.axis_index("seq")
    core = seq % 2
    z = seq // 2
    n_z = n_seq // 2
    partner = z * 2 + 1 - core
    nxt = (seq + 1) % n_seq
    prv = (seq + n_seq - 1) % n_seq
    other = core * nxt + (1 - core) * prv

    barrier = pltpu.get_barrier_semaphore()
    peers = [(d, partner), (d, other)]
    peers += [((d + k) % n_dp, seq) for k in range(1, n_dp)]
    peers += [(d, (z + k) % n_z * 2 + core) for k in range(1, n_z)]
    for peer in peers:
        pl.semaphore_signal(barrier, inc=1, device_id=peer, device_id_type=MESH)
    pl.semaphore_wait(barrier, len(peers))

    def remote(src, dst, send, recv, device):
        return pltpu.make_async_remote_copy(
            src_ref=src, dst_ref=dst, send_sem=send, recv_sem=recv,
            device_id=device, device_id_type=MESH,
        )

    n_taps, depth, width = taps_ref.shape
    half = width // 2
    side = math.isqrt(n_dp)
    a = (1 - core) * (d % side) + core * (d // side)
    b = (1 - core) * (d // side) + core * (d % side)

    def place(ai, bi, which):
        return (1 - which) * (bi * side + ai) + which * (ai * side + bi)

    def shard(owner, which):
        rows = pl.ds(pl.multiple_of(owner * depth, 16), depth)
        return taps.at[:, rows, pl.ds(pl.multiple_of(which * half, 128), half)]

    own_half = taps_ref.at[:, :, pl.ds(pl.multiple_of(core * half, 128), half)]
    tap_copies = []
    for k in range(1, side):
        c = remote(own_half, shard(d, core), tap_send.at[k, 0, 0], tap_recv.at[side - k, 0],
                   (place((a + k) % side, b, core), seq))
        c.start()
        tap_copies.append(c)
        c = remote(own_half, shard(d, core), tap_send.at[0, 0, k], tap_recv.at[0, side - k],
                   (place(a, (b + k) % side, core), seq))
        c.start()
        tap_copies.append(c)
    own_copy = pltpu.make_async_copy(
        taps_ref, taps.at[:, pl.ds(pl.multiple_of(d * depth, 16), depth), :], own_sem)
    own_copy.start()

    length = x_ref.shape[0]
    tokens = length // POOL
    groups = x_ref.shape[1] // LANES

    def activate_rows(i, carry):
        rows = pl.multiple_of(i * 64, 64)
        wide = x_ref[pl.ds(rows, 64), :].astype(F32)
        normal = layer_norm(wide)
        active = normal * jax.nn.sigmoid(1.702 * normal)
        for q in range(groups):
            x_wide[q, pl.ds(rows, 64), :] = wide[:, q * LANES : (q + 1) * LANES]
            act[q, pl.ds(rows + 8, 64), :] = active[:, q * LANES : (q + 1) * LANES]
        return carry

    lax.fori_loop(0, length // 64, activate_rows, 0)
    to_next = remote(act.at[:, pl.ds(length, 8)], act.at[:, pl.ds(0, 8)], halo_send.at[0],
                     halo_recv.at[0], (d, nxt))
    to_prev = remote(act.at[:, pl.ds(8, 8)], act.at[:, pl.ds(length + 8, 8)], halo_send.at[1],
                     halo_recv.at[1], (d, prv))
    to_next.start()
    to_prev.start()
    sens = sens_ref[...]
    readout = read_ref[...]
    heads_grad = dot_last(sens, readout).astype(BF16)
    to_next.wait()
    to_prev.wait()
    act[:, 0:8, :] = jnp.where(seq == 0, 0.0, act[:, 0:8, :])
    act[:, length + 8 : length + 16, :] = jnp.where(
        seq == n_seq - 1, 0.0, act[:, length + 8 : length + 16, :])
    margin = n_taps // 2
    for j in range(POOL + 2 * margin):
        for q in range(groups):
            phases[j * tokens : (j + 1) * tokens, q * LANES : (q + 1) * LANES] = act[
                q, pl.ds(8 - margin + j, tokens, stride=POOL), :].astype(BF16)

    core_copies = []

    def pass_on(i, j):
        owner = place((a + i) % side, (b + j) % side, core)
        piece = shard(owner, core)
        remote(piece, piece, tap_send.at[0, 0, 0], tap_recv.at[i, j], (d, partner)).wait_recv()
        if j == 0:
            for k in range(1, side):
                c = remote(piece, piece, tap_send.at[0, i, k], tap_recv.at[i, side - k],
                           (place(a, (b + k) % side, core), seq))
                c.start()
                tap_copies.append(c)
        c = remote(piece, piece, tap_core_send.at[i, j], tap_core_recv.at[i, j], (d, partner))
        c.start()
        core_copies.append(c)

    order = [(i, j) for j in range(side) for i in range(side) if (i, j) != (0, 0)]
    for i, j in order:
        pass_on(i, j)
    own_copy.wait()
    for c in core_copies:
        c.wait_recv()

    channels = phases.shape[1]
    step = 256
    for lo in range(0, width, step):
        total = dot(phases[0:length, :], taps[0, :, lo : lo + step])
        for t in range(1, n_taps):
            total = total + dot(
                phases[t * tokens : t * tokens + length, :], taps[t, :, lo : lo + step])
        best = None
        for j in range(POOL):
            parts = [x_wide[q, pl.ds(j, tokens, stride=POOL), :]
                     for q in range(lo // LANES, (lo + step) // LANES)]
            item = total[j * tokens : (j + 1) * tokens, :] + jnp.concatenate(parts, axis=1)
            best = item if best is None else jnp.maximum(best, item)
        pooled_ref[:, lo : lo + step] = best.astype(BF16)

    normed = layer_norm(pooled_ref[...].astype(F32)).astype(BF16)
    heads = gain_ref.shape[0]
    probe_width = ask_ref.shape[1]
    value_width = content_ref.shape[1]
    probe = probe_width // heads
    probe_masks = head_masks(tokens, probe_width, heads)
    value_masks = head_masks(tokens, value_width, heads)

    def head_factor(values):
        sums = head_sums(values * values, probe_masks)
        return spread([lax.rsqrt(s * (1.0 / probe) + head_eps) for s in sums], probe_masks)

    keys = dot(normed, look_ref[...])
    kv[seq, :, :probe_width] = (keys * head_factor(keys)).astype(BF16)
    kv[seq, :, probe_width:] = dot(normed, content_ref[...]).astype(BF16)

    def slot(chip, which):
        return kv.at[chip * 2 + which]

    def to_core(chip, index):
        piece = slot(chip, core)
        return remote(piece, piece, kv_core_send.at[index], kv_core_recv.at[index], (d, partner))

    def up(s):
        piece = slot(jnp.maximum(z - s, 0), core)
        return remote(piece, piece, kv_send.at[0, s], kv_recv.at[0, s],
                      (d, (z + 1) % n_z * 2 + core))

    def down(s):
        piece = slot(jnp.minimum(z + s, n_z - 1), core)
        return remote(piece, piece, kv_send.at[1, s], kv_recv.at[1, s],
                      (d, (z + n_z - 1) % n_z * 2 + core))

    @pl.when(z + 1 < n_z)
    def _():
        up(0).start()

    @pl.when(z >= 1)
    def _():
        down(0).start()

    to_core(z, 0).start()

    queries = dot(normed, ask_ref[...])
    query_factor = head_factor(queries)
    query_hat = queries * query_factor
    query_unit = query_hat.astype(BF16)

    for s in range(1, n_z):
        @pl.when(z - s >= 0)
        def _():
            up(s - 1).wait_recv()

            @pl.when(z + 1 < n_z)
            def _():
                up(s).start()

            to_core(jnp.maximum(z - s, 0), s).start()

        @pl.when(z + s < n_z)
        def _():
            down(s - 1).wait_recv()

            @pl.when(z >= 1)
            def _():
                down(s).start()

            to_core(jnp.minimum(z + s, n_z - 1), n_z - 1 + s).start()

    to_core(z, 0).wait()
    for s in range(1, n_z):
        @pl.when(z - s >= 0)
        def _():
            to_core(jnp.maximum(z - s, 0), s).wait()

            @pl.when(z + 1 < n_z)
            def _():
                up(s).wait_send()

        @pl.when(z + s < n_z)
        def _():
            to_core(jnp.minimum(z + s, n_z - 1), n_z - 1 + s).wait()

            @pl.when(z >= 1)
            def _():
                down(s).wait_send()

    @pl.when(z + 1 < n_z)
    def _():
        up(0).wait_send()

    @pl.when(z >= 1)
    def _():
        down(0).wait_send()

    every = n_seq * tokens
    key_all = kv[:, :, :probe_width].reshape(every, probe_width)
    value_all = kv[:, :, probe_width:].reshape(every, value_width)
    heads_out = jnp.zeros((tokens, value_width), F32)
    unit_grad = jnp.zeros((tokens, probe_width), F32)
    zero = jnp.zeros((), BF16)
    for h in range(heads):
        gain = gain_ref[h] * (1.0 / probe)
        scores = dot_last(jnp.where(probe_masks[h], query_unit, zero), key_all) * gain
        expo = jnp.exp(scores)
        probs = expo * (1.0 / jnp.sum(expo, axis=1, keepdims=True))
        head_out = dot(probs.astype(BF16), value_all)
        heads_out = jnp.where(value_masks[h], head_out, heads_out)
        grad_part = jnp.where(value_masks[h], heads_grad, zero)
        prob_grad = dot_last(grad_part, value_all)
        delta = jnp.sum(grad_part.astype(F32) * head_out, axis=1, keepdims=True)
        score_grad = (probs * (prob_grad - delta)).astype(BF16)
        unit_grad = jnp.where(probe_masks[h], dot(score_grad, key_all) * gain, unit_grad)
    heads_low = heads_out.astype(BF16)
    means = [s * (1.0 / probe) for s in head_sums(query_hat * unit_grad, probe_masks)]
    query_diff = (query_factor * (unit_grad - query_hat * spread(means, probe_masks))).astype(BF16)

    block = probe_width
    grads[0:channels, :] = dot_first(normed, query_diff)
    out_local = dot_first(heads_low, sens)
    base = channels
    for lo in range(0, width, block):
        grads[base : base + value_width, :] = out_local[:, lo : lo + block]
        base += value_width
    if base < grads.shape[0]:
        grads[base:, :] = jnp.zeros((grads.shape[0] - base, block), F32)
    core_rows = n_dp * n_z * part
    dp_rows = n_z * part

    def rows_of(start, count):
        return pl.ds(pl.multiple_of(start, 16), count)

    mine = rows_of(core * core_rows, core_rows)
    theirs = rows_of((1 - core) * core_rows, core_rows)
    grads_low[...] = grads[theirs, :].astype(BF16)
    swap = remote(grads_low, from_core, core_send.at[0], core_recv.at[0], (d, partner))
    swap.start()
    update_ref[...] = dot(heads_low, readout)
    swap.wait()
    sums = grads[mine, :] + from_core[...].astype(F32)
    grads[0:core_rows, :] = sums
    low_dp[...] = sums.astype(BF16)
    copies = []
    for k in range(1, n_dp):
        peer = (d + k) % n_dp
        c = remote(low_dp.at[rows_of(peer * dp_rows, dp_rows)], from_dp.at[n_dp - k],
                   dp_send.at[0, k], dp_recv.at[0, n_dp - k], (peer, seq))
        c.start()
        copies.append(c)
    for c in copies:
        c.wait()
    sums = grads[rows_of(d * dp_rows, dp_rows), :]
    for k in range(1, n_dp):
        sums = sums + from_dp[k].astype(F32)
    grads[0:dp_rows, :] = sums
    low_z[...] = sums.astype(BF16)
    copies = []
    for k in range(1, n_z):
        peer = (z + k) % n_z
        c = remote(low_z.at[rows_of(peer * part, part)], from_z.at[n_z - k],
                   z_send.at[0, k], z_recv.at[0, n_z - k], (d, peer * 2 + core))
        c.start()
        copies.append(c)
    for c in copies:
        c.wait()
    sums = grads[rows_of(z * part, part), :]
    for k in range(1, n_z):
        sums = sums + from_z[k].astype(F32)
    first = core * core_rows + d * dp_rows
    own = rows_of(first + z * part, part)
    result[own, :] = sums.astype(BF16)
    copies = []
    for k in range(1, n_z):
        c = remote(result.at[own], result.at[own], z_send.at[1, k], z_recv.at[1, n_z - k],
                   (d, (z + k) % n_z * 2 + core))
        c.start()
        copies.append(c)
    for c in copies:
        c.wait()
    own = rows_of(first, dp_rows)
    copies = []
    for k in range(1, n_dp):
        c = remote(result.at[own], result.at[own], dp_send.at[1, k], dp_recv.at[1, n_dp - k],
                   ((d + k) % n_dp, seq))
        c.start()
        copies.append(c)
    for c in copies:
        c.wait()
    swap = remote(result.at[mine], result.at[mine], core_send.at[1], core_recv.at[1], (d, partner))
    swap.start()
    for c in tap_copies:
        c.wait_send()
    for c in core_copies:
        c.wait_send()
    swap.wait()
    grads_ref[...] = result[...]


def on_device(n_dp, n_seq, x, taps, ask, look, content, read, gain, sens):
    x = x[0]
    sens = sens[0]
    length, channels = x.shape
    n_taps, depth, width = taps.shape
    tokens = length // POOL
    probe_width = ask.shape[1]
    value_width = content.shape[1]
    n_z = n_seq // 2
    side = math.isqrt(n_dp)
    devices = n_dp * n_seq
    real_rows = channels + value_width * (width // probe_width)
    part = -(-real_rows // (devices * 16)) * 16
    total_rows = part * devices
    core_rows = total_rows // 2
    dp_rows = core_rows // n_dp
    vmem = pl.BlockSpec(memory_space=pltpu.VMEM)
    dma = pltpu.SemaphoreType.DMA
    pooled, update, grads = pl.pallas_call(
        functools.partial(kernel, n_dp, n_seq, part),
        out_shape=(
            jax.ShapeDtypeStruct((tokens, width), BF16),
            jax.ShapeDtypeStruct((tokens, width), F32),
            jax.ShapeDtypeStruct((total_rows, probe_width), BF16),
        ),
        in_specs=[
            vmem, pl.BlockSpec(memory_space=pl.ANY), vmem, vmem, vmem, vmem,
            pl.BlockSpec(memory_space=pltpu.SMEM), vmem,
        ],
        out_specs=(vmem, vmem, vmem),
        scratch_shapes=[
            pltpu.VMEM((n_taps, channels, width), BF16),
            pltpu.VMEM((channels // LANES, length, LANES), F32),
            pltpu.VMEM((channels // LANES, length + 16, LANES), F32),
            pltpu.VMEM(((POOL + 2 * (n_taps // 2)) * tokens, channels), BF16),
            pltpu.VMEM((n_seq, tokens, probe_width + value_width), BF16),
            pltpu.VMEM((total_rows, probe_width), F32),
            pltpu.VMEM((core_rows, probe_width), BF16),
            pltpu.VMEM((core_rows, probe_width), BF16),
            pltpu.VMEM((n_dp, dp_rows, probe_width), BF16),
            pltpu.VMEM((n_z, part, probe_width), BF16),
            pltpu.VMEM((core_rows, probe_width), BF16),
            pltpu.VMEM((dp_rows, probe_width), BF16),
            pltpu.VMEM((total_rows, probe_width), BF16),
            dma((side, side, side)),
            dma((side, side)),
            dma((side, side)),
            dma((side, side)),
            dma,
            dma((2,)),
            dma((2,)),
            dma((2, n_z)),
            dma((2, n_z)),
            dma((2 * n_z,)),
            dma((2 * n_z,)),
            dma((2, n_dp)),
            dma((2, n_dp)),
            dma((2, n_z)),
            dma((2, n_z)),
            dma((2,)),
            dma((2,)),
        ],
        compiler_params=pltpu.CompilerParams(
            collective_id=0, has_side_effects=True, vmem_limit_bytes=58 * 1024 * 1024
        ),
    )(x, taps, ask, look, content, read, gain, sens)
    query_grad = grads[:channels].astype(F32)
    blocks = grads[channels:real_rows].reshape(width // probe_width, value_width, probe_width)
    out_grad = jnp.concatenate(list(blocks), axis=1).astype(F32)
    return pooled[None], update[None], query_grad, out_grad


def solution(mesh):
    return jax.shard_map(
        functools.partial(on_device, mesh.shape["dp"], mesh.shape["seq"]),
        mesh=mesh,
        in_specs=(
            P("dp", "seq", None),
            P(None, "dp", None),
            P(),
            P(),
            P(),
            P(),
            P(),
            P("dp", "seq", None),
        ),
        out_specs=(P("dp", "seq", None), P("dp", "seq", None), P(), P()),
        check_vma=False,
    )
```

time: 279 us -> 96.5 us (0.35)
  waiting for transfers between devices: 191 us -> 0 us
  Pallas kernels: 0 us -> 90.1 us
  blocking collectives: 30.7 us -> 0 us
  matrix products: 21.7 us -> 0 us
  between operations: 17 us -> 0.65 us
  other arithmetic: 10.2 us -> 3.02 us
  starting transfers between devices: 3.72 us -> 0 us
    psum x1 -> x0, waiting for transfers between devices: 133 us -> none  [on_device(): query_grad, out_grad = lax.psum((query_local, out_local), ('dp', 'seq'))]
    pallas_call x0 -> x1, Pallas kernels: none -> 90.1 us  [on_device(): pl.pallas_call(functools.partial(kernel, n_dp, n_seq, part), out_shape=(j...]
    all_gather x1 -> x0, waiting for transfers between devices: 56.6 us -> none  [on_device(): all_taps = lax.all_gather(kernel_coefficients, 'dp', axis=1, tiled=True)]
    all_gather x2 -> x0, blocking collectives: 30.7 us -> none  [the longest x1 15.8 us: on_device(): lax.all_gather(value_local, 'seq', axis=0, tiled=True)]
    dot_general x20 -> x0, matrix products: 21.7 us -> none  [the longest x1 7.07 us: stacked_conv(): return jnp.dot(windows, flat_taps, preferred_element_type=jnp.float32)]
    unnamed x4 -> x0, other arithmetic: 4.91 us -> none
    ppermute x2 -> x0, starting transfers between devices: 3.65 us -> none  [the longest x1 2.36 us: padded_2(): before = lax.ppermute(last, axis, up)]
  transfers between devices with their start and end apart: 4 -> 0, of which waited for: 2 -> 0; matrix products, arithmetic and copies ran while one was open for 3% -> 0% of each run, Pallas kernels for 0% -> 0%
where the time goes in v1:
time: 96.5 us; the launch traced here: 96.3 us
  Pallas kernels  90.1 us (93%)
  other arithmetic  3.02 us (3%)
  local copies, waits for them, and re-layouts  2.59 us (3%)
    pallas_call x1, Pallas kernels, on_device(): pl.pallas_call(functools.partial(kernel, n_dp, n_seq, part), out_shape=(j...  90.1 us
    convert_element_type x1, other arithmetic, on_device(): query_grad = grads[:channels].astype(F32)  1.93 us

profile of v1, /device:TPU:0, one launch (start us, length us, event | category | flops | bytes accessed | tf_op | source)
XLA Modules:
  0.0 96.3 jit_solution(5227513474729786282)
XLA Ops:
  0.6 90.1 %shard_map.111 = (bf16[128,768]{1,0:T(8,128)(2,1)}, f32[128,768]{1,0:T(8,128)}, bf16[2048,256]{1,0:T(8,128)(2,1)}) custom-call(bf16[512,768]{1,0:T(8,128)(2,1)} %bitcast.4, bf16[5,192,768]{2,1,0:T(8,128)(2,1)} %taps_ref.1, bf16[768,256]{1,0:T(8,128)(2,1)} %ask_ref.1, bf16[768,256]{1,0:T(8,128)(2,1)} %look_ref.1, bf16[768,384]{1,0:T(8,128)(2,1)} %content_ref.1, ...), custom_call_target="tpu_custom_call" | custom-call | tf_op jit(solution)/shard_map/pallas_call | solution.py:443
  90.7 1.2 %fusion = (bf16[384,256]{1,0:T(8,128)(2,1)S(1)}, bf16[384,256]{1,0:T(8,128)(2,1)S(1)}, bf16[384,256]{1,0:T(8,128)(2,1)S(1)}) fusion(bf16[2048,256]{1,0:T(8,128)(2,1)} %get-tuple-element.9), kind=kLoop, calls=%fused_computation.2 | loop fusion | bytes 1179648 | tf_op jit(solution)/shard_map/unstack | solution.py:493
  91.9 1.9 %slice_convert_fusion = f32[768,256]{1,0:T(8,128)} fusion(bf16[2048,256]{1,0:T(8,128)(2,1)} %get-tuple-element.9), kind=kLoop, calls=%fused_computation.1 | loop fusion | flops 196608 | bytes 1179648 | tf_op jit(solution)/shard_map/convert_element_type | solution.py:491
  93.8 0.0 copy-start.1
  93.8 0.0 copy-start
  93.8 1.1 %maximum_convert_fusion = f32[384,768]{1,0:T(8,128)} fusion(bf16[384,256]{1,0:T(8,128)(2,1)S(1)} %get-tuple-element.11, bf16[384,256]{1,0:T(8,128)(2,1)S(1)} %get-tuple-element.12, bf16[384,256]{1,0:T(8,128)(2,1)S(1)} %get-tuple-element.10), kind=kLoop, calls=%fused_computation | loop fusion | flops 1769472 | bytes 1769472 | tf_op jit(solution)/shard_map/convert_element_type | solution.py:493
  94.9 0.0 copy-done.1
  94.9 0.7 copy.14
  95.6 0.0 copy-done
  95.6 0.7 copy.15
Async XLA Ops:
  93.8 1.1 %copy-start.1 = (bf16[128,768]{1,0:T(8,128)(2,1)S(1)}, bf16[128,768]{1,0:T(8,128)(2,1)}, u32[]{:S(2)}) copy-start(bf16[128,768]{1,0:T(8,128)(2,1)} %get-tuple-element.7) | copy-start | bytes 589828
  93.8 1.8 %copy-start = (f32[128,768]{1,0:T(8,128)S(1)}, f32[128,768]{1,0:T(8,128)}, u32[]{:S(2)}) copy-start(f32[128,768]{1,0:T(8,128)} %get-tuple-element.8) | copy-start | bytes 1179652

commit v2 on v1

--- a/solution.py
+++ b/solution.py
@@ -85,6 +85,8 @@
     tap_recv,
     tap_core_send,
     tap_core_recv,
+    tap_z_send,
+    tap_z_recv,
     own_sem,
     halo_send,
     halo_recv,
@@ -109,6 +111,22 @@
     prv = (seq + n_seq - 1) % n_seq
     other = core * nxt + (1 - core) * prv
 
+    n_taps, depth, width = taps_ref.shape
+    n_blocks = taps.shape[1]
+    cols = width // n_blocks
+
+    def rows_of(start, count):
+        return pl.ds(pl.multiple_of(start, 16), count)
+
+    own_copies = [
+        pltpu.make_async_copy(
+            taps_ref.at[:, :, m * cols : (m + 1) * cols],
+            taps.at[:, m, rows_of(d * depth, depth), :], own_sem.at[m])
+        for m in range(n_blocks)
+    ]
+    for c in own_copies:
+        c.start()
+
     barrier = pltpu.get_barrier_semaphore()
     peers = [(d, partner), (d, other)]
     peers += [((d + k) % n_dp, seq) for k in range(1, n_dp)]
@@ -123,8 +141,6 @@
             device_id=device, device_id_type=MESH,
         )
 
-    n_taps, depth, width = taps_ref.shape
-    half = width // 2
     side = math.isqrt(n_dp)
     a = (1 - core) * (d % side) + core * (d // side)
     b = (1 - core) * (d // side) + core * (d % side)
@@ -132,24 +148,57 @@
     def place(ai, bi, which):
         return (1 - which) * (bi * side + ai) + which * (ai * side + bi)
 
-    def shard(owner, which):
-        rows = pl.ds(pl.multiple_of(owner * depth, 16), depth)
-        return taps.at[:, rows, pl.ds(pl.multiple_of(which * half, 128), half)]
-
-    own_half = taps_ref.at[:, :, pl.ds(pl.multiple_of(core * half, 128), half)]
+    parity = z % 2
+    pair = z + 1 - 2 * parity
+    thirds = [1 + parity, 0, 2 - parity]
+
+    def piece(owner, u):
+        return taps.at[:, thirds[u] * 2 + core, rows_of(owner * depth, depth), :]
+
     tap_copies = []
-    for k in range(1, side):
-        c = remote(own_half, shard(d, core), tap_send.at[k, 0, 0], tap_recv.at[side - k, 0],
-                   (place((a + k) % side, b, core), seq))
-        c.start()
-        tap_copies.append(c)
-        c = remote(own_half, shard(d, core), tap_send.at[0, 0, k], tap_recv.at[0, side - k],
-                   (place(a, (b + k) % side, core), seq))
-        c.start()
-        tap_copies.append(c)
-    own_copy = pltpu.make_async_copy(
-        taps_ref, taps.at[:, pl.ds(pl.multiple_of(d * depth, 16), depth), :], own_sem)
-    own_copy.start()
+    core_copies = {}
+
+    def direct(u):
+        own = piece(d, u)
+        for k in range(1, side):
+            tap_copies.append(remote(
+                own, own, tap_send.at[u, 0, 0, k], tap_recv.at[u, side - k, 0],
+                (place((a + k) % side, b, core), seq)))
+            tap_copies[-1].start()
+            tap_copies.append(remote(
+                own, own, tap_send.at[u, 1, 0, k], tap_recv.at[u, 0, side - k],
+                (place(a, (b + k) % side, core), seq)))
+            tap_copies[-1].start()
+
+    def owner_of(i, j):
+        return place((a + i) % side, (b + j) % side, core)
+
+    def cross(u, i, j):
+        own = piece(owner_of(i, j), u)
+        core_copies[u, i, j] = remote(
+            own, own, tap_core_send.at[u, i, j], tap_core_recv.at[u, i, j], (d, partner))
+        core_copies[u, i, j].start()
+
+    z_copies = {}
+
+    def pass_on(u, i, j):
+        own = piece(owner_of(i, j), u)
+        remote(own, own, tap_send.at[u, 0, 0, 0], tap_recv.at[u, i, j], (d, partner)).wait_recv()
+        if j == 0:
+            for k in range(1, side):
+                tap_copies.append(remote(
+                    own, own, tap_send.at[u, 1, i, k], tap_recv.at[u, i, side - k],
+                    (place(a, (b + k) % side, core), seq)))
+                tap_copies[-1].start()
+        if u == 0:
+            z_copies[i, j] = remote(
+                own, own, tap_z_send.at[i, j], tap_z_recv.at[i, j], (d, pair * 2 + core))
+            z_copies[i, j].start()
+        cross(u, i, j)
+
+    for c in own_copies:
+        c.wait()
+    direct(0)
 
     length = x_ref.shape[0]
     tokens = length // POOL
@@ -186,43 +235,50 @@
             phases[j * tokens : (j + 1) * tokens, q * LANES : (q + 1) * LANES] = act[
                 q, pl.ds(8 - margin + j, tokens, stride=POOL), :].astype(BF16)
 
-    core_copies = []
-
-    def pass_on(i, j):
-        owner = place((a + i) % side, (b + j) % side, core)
-        piece = shard(owner, core)
-        remote(piece, piece, tap_send.at[0, 0, 0], tap_recv.at[i, j], (d, partner)).wait_recv()
-        if j == 0:
-            for k in range(1, side):
-                c = remote(piece, piece, tap_send.at[0, i, k], tap_recv.at[i, side - k],
-                           (place(a, (b + k) % side, core), seq))
-                c.start()
-                tap_copies.append(c)
-        c = remote(piece, piece, tap_core_send.at[i, j], tap_core_recv.at[i, j], (d, partner))
-        c.start()
-        core_copies.append(c)
-
-    order = [(i, j) for j in range(side) for i in range(side) if (i, j) != (0, 0)]
-    for i, j in order:
-        pass_on(i, j)
-    own_copy.wait()
-    for c in core_copies:
-        c.wait_recv()
-
+    first = [(i, 0) for i in range(1, side)]
+    second = [(0, j) for j in range(1, side)]
+    third = [(i, j) for j in range(1, side) for i in range(1, side)]
     channels = phases.shape[1]
-    step = 256
-    for lo in range(0, width, step):
-        total = dot(phases[0:length, :], taps[0, :, lo : lo + step])
-        for t in range(1, n_taps):
-            total = total + dot(
-                phases[t * tokens : t * tokens + length, :], taps[t, :, lo : lo + step])
+
+    def convolve(u):
+        for at in first + second + third:
+            core_copies[(u,) + at].wait_recv()
+        step = 2 * cols
+        lo = thirds[u] * 2
+        total = None
+        for t in range(n_taps):
+            weight = jnp.concatenate([taps[t, lo], taps[t, lo + 1]], axis=1)
+            term = dot(phases[t * tokens : t * tokens + length, :], weight)
+            total = term if total is None else total + term
         best = None
         for j in range(POOL):
-            parts = [x_wide[q, pl.ds(j, tokens, stride=POOL), :]
-                     for q in range(lo // LANES, (lo + step) // LANES)]
+            rows = pl.ds(j, tokens, stride=POOL)
+            parts = [x_wide[thirds[u] * (step // LANES) + q, rows, :] for q in range(step // LANES)]
             item = total[j * tokens : (j + 1) * tokens, :] + jnp.concatenate(parts, axis=1)
             best = item if best is None else jnp.maximum(best, item)
-        pooled_ref[:, lo : lo + step] = best.astype(BF16)
+        pooled_ref[:, pl.ds(pl.multiple_of(thirds[u] * step, 128), step)] = best.astype(BF16)
+
+    for i, j in first + second:
+        pass_on(0, i, j)
+    direct(1)
+    for i, j in third:
+        pass_on(0, i, j)
+    for i, j in first + second:
+        pass_on(1, i, j)
+    convolve(0)
+
+    def from_pair(i, j):
+        z_copies[i, j].wait_recv()
+        cross(2, i, j)
+
+    for i, j in third:
+        pass_on(1, i, j)
+    for i, j in first + second:
+        from_pair(i, j)
+    convolve(1)
+    for i, j in third:
+        from_pair(i, j)
+    convolve(2)
 
     normed = layer_norm(pooled_ref[...].astype(F32)).astype(BF16)
     heads = gain_ref.shape[0]
@@ -352,9 +408,6 @@
         grads[base:, :] = jnp.zeros((grads.shape[0] - base, block), F32)
     core_rows = n_dp * n_z * part
     dp_rows = n_z * part
-
-    def rows_of(start, count):
-        return pl.ds(pl.multiple_of(start, 16), count)
 
     mine = rows_of(core * core_rows, core_rows)
     theirs = rows_of((1 - core) * core_rows, core_rows)
@@ -416,10 +469,22 @@
     swap.start()
     for c in tap_copies:
         c.wait_send()
-    for c in core_copies:
+    for c in list(core_copies.values()) + list(z_copies.values()):
         c.wait_send()
     swap.wait()
     grads_ref[...] = result[...]
+
+
+def finish(pooled_in, update_in, grads_in, pooled_ref, update_ref, query_ref, out_ref):
+    pooled_ref[...] = pooled_in[...]
+    update_ref[...] = update_in[...]
+    base = query_ref.shape[0]
+    query_ref[...] = grads_in[0:base, :].astype(F32)
+    rows, width = out_ref.shape
+    block = query_ref.shape[1]
+    for lo in range(0, width, block):
+        out_ref[:, lo : lo + block] = grads_in[base : base + rows, :].astype(F32)
+        base += rows
 
 
 def on_device(n_dp, n_seq, x, taps, ask, look, content, read, gain, sens):
@@ -438,6 +503,7 @@
     total_rows = part * devices
     core_rows = total_rows // 2
     dp_rows = core_rows // n_dp
+    blocks = 6
     vmem = pl.BlockSpec(memory_space=pltpu.VMEM)
     dma = pltpu.SemaphoreType.DMA
     pooled, update, grads = pl.pallas_call(
@@ -453,7 +519,7 @@
         ],
         out_specs=(vmem, vmem, vmem),
         scratch_shapes=[
-            pltpu.VMEM((n_taps, channels, width), BF16),
+            pltpu.VMEM((n_taps, blocks, channels, width // blocks), BF16),
             pltpu.VMEM((channels // LANES, length, LANES), F32),
             pltpu.VMEM((channels // LANES, length + 16, LANES), F32),
             pltpu.VMEM(((POOL + 2 * (n_taps // 2)) * tokens, channels), BF16),
@@ -466,11 +532,13 @@
             pltpu.VMEM((core_rows, probe_width), BF16),
             pltpu.VMEM((dp_rows, probe_width), BF16),
             pltpu.VMEM((total_rows, probe_width), BF16),
-            dma((side, side, side)),
+            dma((2, 2, side, side)),
+            dma((2, side, side)),
+            dma((3, side, side)),
+            dma((3, side, side)),
             dma((side, side)),
             dma((side, side)),
-            dma((side, side)),
-            dma,
+            dma((blocks,)),
             dma((2,)),
             dma((2,)),
             dma((2, n_z)),
@@ -488,9 +556,18 @@
             collective_id=0, has_side_effects=True, vmem_limit_bytes=58 * 1024 * 1024
         ),
     )(x, taps, ask, look, content, read, gain, sens)
-    query_grad = grads[:channels].astype(F32)
-    blocks = grads[channels:real_rows].reshape(width // probe_width, value_width, probe_width)
-    out_grad = jnp.concatenate(list(blocks), axis=1).astype(F32)
+    pooled, update, query_grad, out_grad = pl.pallas_call(
+        finish,
+        out_shape=(
+            jax.ShapeDtypeStruct((tokens, width), BF16),
+            jax.ShapeDtypeStruct((tokens, width), F32),
+            jax.ShapeDtypeStruct((channels, probe_width), F32),
+            jax.ShapeDtypeStruct((value_width, width), F32),
+        ),
+        in_specs=[vmem, vmem, vmem],
+        out_specs=(vmem, vmem, vmem, vmem),
+        compiler_params=pltpu.CompilerParams(vmem_limit_bytes=40 * 1024 * 1024),
+    )(pooled, update, grads)
     return pooled[None], update[None], query_grad, out_grad
 
 

time: 96.5 us -> 90.5 us (0.938)
  Pallas kernels: 90.1 us -> 86.4 us
  other arithmetic: 3.02 us -> 0 us
    pallas_call x1, Pallas kernels: 90.1 us -> 84.9 us  [on_device(): pl.pallas_call(functools.partial(kernel, n_dp, n_seq, part), out_shape=(j...]
    convert_element_type x2 -> x0, other arithmetic: 3.02 us -> none  [the longest x1 1.93 us: on_device(): query_grad = grads[:channels].astype(F32)]
    unnamed x6, local copies, waits for them, and re-layouts: 1.43 us -> 3.14 us
    pallas_call x0 -> x1, Pallas kernels: none -> 1.51 us  [on_device(): pl.pallas_call(finish, out_shape=(jax.ShapeDtypeStruct((tokens, width), B...]
    another operation x1 -> x0, local copies, waits for them, and re-layouts: 1.16 us -> none  [on_device(): out_grad = jnp.concatenate(list(blocks), axis=1).astype(F32)]
where the time goes in v2:
time: 90.5 us; the launch traced here: 90.2 us
  Pallas kernels  86.4 us (95%)
  local copies, waits for them, and re-layouts  3.14 us (3%)
    pallas_call x1, Pallas kernels, on_device(): pl.pallas_call(functools.partial(kernel, n_dp, n_seq, part), out_shape=(j...  84.9 us
    unnamed x6, local copies, waits for them, and re-layouts  3.14 us

profile of v2, /device:TPU:0, one launch (start us, length us, event | category | flops | bytes accessed | tf_op | source)
XLA Modules:
  0.0 90.2 jit_solution(10096175013672418000)
XLA Ops:
  0.6 84.9 %shard_map.111 = (bf16[128,768]{1,0:T(8,128)(2,1)}, f32[128,768]{1,0:T(8,128)}, bf16[2048,256]{1,0:T(8,128)(2,1)}) custom-call(bf16[512,768]{1,0:T(8,128)(2,1)} %bitcast.4, bf16[5,192,768]{2,1,0:T(8,128)(2,1)} %taps_ref.1, bf16[768,256]{1,0:T(8,128)(2,1)} %ask_ref.1, bf16[768,256]{1,0:T(8,128)(2,1)} %look_ref.1, bf16[768,384]{1,0:T(8,128)(2,1)} %content_ref.1, ...), custom_call_target="tpu_custom_call" | custom-call | tf_op jit(solution)/shard_map/pallas_call | solution.py:509
  85.6 0.0 copy-start
  85.6 1.2 %copy-done = bf16[2048,256]{1,0:T(8,128)(2,1)S(1)} copy-done((bf16[2048,256]{1,0:T(8,128)(2,1)S(1)}, bf16[2048,256]{1,0:T(8,128)(2,1)}, u32[]{:S(2)}) %copy-start) | copy-done | bytes 1048600
  86.8 0.0 copy-start.1
  86.8 1.0 %copy-done.1 = f32[128,768]{1,0:T(8,128)S(1)} copy-done((f32[128,768]{1,0:T(8,128)S(1)}, f32[128,768]{1,0:T(8,128)}, u32[]{:S(2)}) %copy-start.1) | copy-done | bytes 393240
  87.8 0.0 copy-start.2
  87.8 0.9 %copy-done.2 = bf16[128,768]{1,0:T(8,128)(2,1)S(1)} copy-done((bf16[128,768]{1,0:T(8,128)(2,1)S(1)}, bf16[128,768]{1,0:T(8,128)(2,1)}, u32[]{:S(2)}) %copy-start.2) | copy-done | bytes 196632
  88.7 1.5 %shard_map.112 = (bf16[128,768]{1,0:T(8,128)(2,1)}, f32[128,768]{1,0:T(8,128)}, f32[768,256]{1,0:T(8,128)}, f32[384,768]{1,0:T(8,128)}) custom-call(bf16[128,768]{1,0:T(8,128)(2,1)S(1)} %copy-done.2, f32[128,768]{1,0:T(8,128)S(1)} %copy-done.1, bf16[2048,256]{1,0:T(8,128)(2,1)S(1)} %copy-done), custom_call_target="tpu_custom_call" | custom-call | tf_op jit(solution)/shard_map/pallas_call | solution.py:559
Async XLA Ops:
  85.6 1.2 %copy-start = (bf16[2048,256]{1,0:T(8,128)(2,1)S(1)}, bf16[2048,256]{1,0:T(8,128)(2,1)}, u32[]{:S(2)}) copy-start(bf16[2048,256]{1,0:T(8,128)(2,1)} %get-tuple-element.13.grads_in) | copy-start | bytes 3145732
  86.8 1.0 %copy-start.1 = (f32[128,768]{1,0:T(8,128)S(1)}, f32[128,768]{1,0:T(8,128)}, u32[]{:S(2)}) copy-start(f32[128,768]{1,0:T(8,128)} %get-tuple-element.12.update_in) | copy-start | bytes 1179652
  87.8 0.9 %copy-start.2 = (bf16[128,768]{1,0:T(8,128)(2,1)S(1)}, bf16[128,768]{1,0:T(8,128)(2,1)}, u32[]{:S(2)}) copy-start(bf16[128,768]{1,0:T(8,128)(2,1)} %get-tuple-element.11.pooled_in) | copy-start | bytes 589828
